TPU v7x, 32 devices: a whole 2x2x4 slice. The times are simulated.
32 devices in a mesh: pop: 2 (over y), exp: 16 (over z, x, core), tp: 1.
Axes of the slice: x: 2, y: 2, z: 4, core: 2. Of those that a mesh axis runs over, the one named last changes fastest.
Arguments:
- tokens: bfloat16 [2048, 2880], P(('pop', 'exp'), 'tp'), parts along dimension 0, may hold values from -6 to 6
- routes: int32 [2048, 4], P(('pop', 'exp')), parts along dimension 0, may hold values from 0 to 7, all different within a row; in each aligned block of 64 rows (0 to 63, 64 to 127, ...) at most 64 rows name the same one
- router_weight: bfloat16 [2880, 8], P('tp'), may hold values from -0.109375 to 0.109375
- router_bias: float32 [8], replicated, may hold values from -120 to 163
- member_seeds: int32 [4], P('pop'), parts along dimension 0, may hold values from 0 to 16777215
- gate_weight: bfloat16 [16, 2880, 768], P('exp', None, 'tp'), may hold values from -0.109375 to 0.109375
- up_weight: bfloat16 [16, 2880, 768], P('exp', None, 'tp'), may hold values from -0.109375 to 0.109375
Outputs:
- routed_activations: bfloat16 [2048, 4, 2, 768], P(('pop', 'exp'), None, None, 'tp'), parts along dimension 0
There are 2 independent parts, one for each index of `pop`. A program takes and returns all parts, laid end to end along the dimension named above; an argument that names none is the same for every part. Nothing has to cross between parts.
Inputs may be any that keep to these rules, and one draw needn't show every extreme that they name: `routes`: no expert is named by more than 64 of the 64 rows of one device, and in some device's rows one expert is named exactly 64 times.
All inputs are finite; a program needn't handle non-finite values.
Results may differ from a plain program's by a relative error of at most 0.0049.
Values may be sent and summed in bfloat16 or wider, within the bound.
A program may use at most 64 MiB of HBM per device.

v0:
```python
import math

import jax
import jax.numpy as jnp
from jax import lax
from jax.sharding import PartitionSpec as P

FW = 1536
LENGTH = 512


NOISE = 0.25
ALPHA = 1.702


def noise_table(member_seeds, matrix_tag, expert, positions, expert_count):
    rank_index = jnp.arange(4, dtype=jnp.int32)
    counter = ((matrix_tag * expert_count + expert) * 4 + rank_index) * 4096
    counter = counter[None, None, :] + positions[:, None, None]
    hashed = (member_seeds[None, :, None] * 31 + counter) * 1103515245 + 12345
    hashed = hashed ^ hashed >> 16
    hashed = hashed * 747796405
    levels = (hashed >> 16 & 255) - 128
    return (levels.astype(jnp.float32) / 128.0).reshape(positions.shape[0], -1)


def expert_rows(
    inputs, transcripts, member_seeds, gate_cols, up_cols, expert, hidden_index, expert_count
):
    model_width = inputs.shape[1]
    members = member_seeds.shape[0]
    positions = jnp.arange(model_width, dtype=jnp.int32)
    left_factors = jnp.concatenate(
        [
            noise_table(member_seeds, 0, expert, positions, expert_count),
            noise_table(member_seeds, 1, expert, positions, expert_count),
        ],
        axis=1,
    ).astype(jnp.bfloat16)
    projected = jnp.dot(inputs, left_factors, preferred_element_type=jnp.float32)
    select = (transcripts[:, None] == jnp.arange(members, dtype=jnp.int32)[None, :]).astype(
        jnp.float32
    )
    select = jnp.repeat(select, 4, axis=1)
    noise_scale = NOISE / math.sqrt(model_width)
    gate_noise = jnp.dot(
        projected[:, : 4 * members] * select,
        noise_table(member_seeds, 2, expert, hidden_index, expert_count).T,
        precision=lax.Precision.HIGHEST,
    )
    up_noise = jnp.dot(
        projected[:, 4 * members :] * select,
        noise_table(member_seeds, 3, expert, hidden_index, expert_count).T,
        precision=lax.Precision.HIGHEST,
    )
    gate_sum = (
        jnp.dot(inputs, gate_cols, preferred_element_type=jnp.float32) + noise_scale * gate_noise
    )
    up_sum = jnp.dot(inputs, up_cols, preferred_element_type=jnp.float32) + noise_scale * up_noise
    return (gate_sum * jax.nn.sigmoid(ALPHA * gate_sum) * (up_sum + 1.0)).astype(jnp.bfloat16)


def local(tokens, routes, router_weight, router_bias, member_seeds, gate_weight, up_weight):
    tok_rows = tokens.shape[0]
    top_count = routes.shape[1]
    expert_count = router_weight.shape[1]
    quarter = gate_weight.shape[2]
    capacity = min(tok_rows, max(2, 2 * tok_rows * top_count // expert_count))
    device_count = lax.axis_size("exp")
    home_index = lax.axis_index("exp")
    core_index = lax.axis_index("tp")
    half_index = home_index % 2
    this_expert = home_index // 2
    partial_logits = jnp.dot(tokens, router_weight, preferred_element_type=jnp.float32)
    logits = lax.psum(partial_logits, "tp") + router_bias
    expert_ids = jnp.arange(expert_count, dtype=jnp.int32)
    chosen = jnp.sum(
        jnp.where(routes[:, :, None] == expert_ids[None, None, :], logits[:, None, :], 0.0), axis=2
    )
    weights = jax.nn.softmax(chosen, axis=1)
    flat_routes = routes.reshape(-1)
    entry_count = tok_rows * top_count
    flat_hot = (flat_routes[:, None] == expert_ids[None, :]).astype(jnp.int32)
    slot_index = jnp.sum((jnp.cumsum(flat_hot, axis=0) - 1) * flat_hot, axis=1)
    entry_rows = jnp.arange(entry_count, dtype=jnp.int32) // top_count
    entry_transcript = ((home_index * tok_rows + entry_rows) // LENGTH).astype(jnp.bfloat16)
    features = lax.all_gather(tokens, "tp", axis=1, tiled=True)
    feature_width = features.shape[1]
    entry_features = features[entry_rows]
    destination = jnp.concatenate([2 * flat_routes, 2 * flat_routes + 1])
    position = jnp.concatenate([slot_index, slot_index])
    payload = jnp.concatenate([entry_features, entry_features], axis=0)
    labels = jnp.concatenate([entry_transcript, entry_transcript])
    target = destination * capacity + position
    send_rows = (
        jnp.zeros((device_count * capacity, feature_width), jnp.bfloat16).at[target].set(payload)
    )
    send_rows = send_rows.reshape(device_count, capacity, feature_width)
    send_labels = jnp.full((device_count * capacity,), -1.0, jnp.bfloat16).at[target].set(labels)
    send_labels = send_labels.reshape(device_count, capacity)
    hidden_index = (
        half_index * (FW // 2) + core_index * quarter + jnp.arange(quarter, dtype=jnp.int32)
    )
    arrived_rows = lax.all_to_all(send_rows, "exp", split_axis=0, concat_axis=0, tiled=True)
    arrived_labels = lax.all_to_all(send_labels, "exp", split_axis=0, concat_axis=0, tiled=True)
    flat_rows = arrived_rows.reshape(-1, arrived_rows.shape[-1])
    transcripts = arrived_labels.reshape(-1).astype(jnp.int32)
    activation = expert_rows(
        flat_rows,
        transcripts,
        member_seeds,
        gate_weight[0],
        up_weight[0],
        this_expert,
        hidden_index,
        expert_count,
    )
    activation = activation.reshape(arrived_labels.shape + (quarter,))
    returned = lax.all_to_all(activation, "exp", split_axis=0, concat_axis=0, tiled=True)
    returned = returned.reshape(-1, quarter)
    pick_index = (
        (2 * flat_routes)[:, None] + jnp.arange(2, dtype=jnp.int32)[None, :]
    ) * capacity + slot_index[:, None]
    picked = returned[pick_index]
    routed = (picked.astype(jnp.float32) * weights.reshape(-1)[:, None, None]).astype(jnp.bfloat16)
    return routed.reshape(tok_rows, top_count, 2, quarter)


def solution(mesh):
    in_specs = (
        P(("pop", "exp"), "tp"),
        P(("pop", "exp"), None),
        P("tp", None),
        P(),
        P("pop"),
        P("exp", None, "tp"),
        P("exp", None, "tp"),
    )
    out_specs = P(("pop", "exp"), None, None, "tp")
    return jax.shard_map(local, mesh=mesh, in_specs=in_specs, out_specs=out_specs, check_vma=False)
```

profile of v0, /device:TPU:3, one launch (start us, length us, event | category | flops | bytes accessed | tf_op | source)
XLA Modules:
  0.0 232.8 jit_solution(17501408172241623260)
XLA Ops:
  0.0 0.0 copy-start
  0.0 0.8 copy.19
  0.8 0.1 eq.54
  0.9 0.1 reshape.399
  1.1 0.6 reduce-window.6
  1.6 0.2 slice_reduce_fusion
  1.9 0.1 fusion.64
  2.0 3.8 %scatter_custom_fusion.1 = bf16[1024]{0:T(1024)(128)(2,1)S(1)} fusion(s32[512]{0:T(512)S(1)} %bitcast.43, bf16[512]{0:T(512)(128)(2,1)S(1)} %pad_maximum_fusion, bf16[]{:T(256)} %constant.123.clone.1), kind=kCustom, calls=%fused_computation.115 | custom fusion | bytes 2050 | tf_op jit(solution)/shard_map/scatter | solution.py:99
  5.8 0.7 all_to_all.16
  6.5 6.7 %all-to-all-start.1 = ((bf16[16,1,64]{2,1,0:T(2,128)(2,1)}), bf16[16,1,64]{2,1,0:T(2,128)(2,1)S(1)}, u32[]{:S(2)}, u32[]{:S(2)}) async-start(bf16[16,1,64]{2,1,0:T(2,128)(2,1)} %all_to_all.16), calls=%async_computation.1 | async-start | bytes 16384 | tf_op jit(solution)/shard_map/all_to_all | solution.py:105
  13.2 0.0 copy-done
  13.2 1.6 gather_fusion
  14.8 8.3 %scatter_custom_fusion = bf16[1024,2880]{1,0:T(8,128)(2,1)} fusion(s32[512]{0:T(512)S(1)} %bitcast.44, bf16[256,2880]{1,0:T(8,128)(2,1)S(1)} %gather_fusion, bf16[]{:T(256)} %constant.138, bf16[]{:T(256)} %constant.54.clone.1), kind=kCustom, calls=%fused_computation.9 | custom fusion | flops 5898240 | bytes 7405572 | tf_op jit(solution)/shard_map/scatter | solution.py:96
  23.2 0.0 all-to-all-done.1
  23.2 0.0 copy-start.3
  23.2 6.2 %all-to-all-start = ((bf16[16,64,2880]{2,1,0:T(8,128)(2,1)}), bf16[16,64,2880]{2,1,0:T(8,128)(2,1)}, u32[]{:S(2)}, u32[]{:S(2)}) async-start(bf16[16,64,2880]{2,1,0:T(8,128)(2,1)} %bitcast.39), calls=%async_computation | async-start | bytes 12058624 | tf_op jit(solution)/shard_map/all_to_all | solution.py:104
  29.3 0.1 iota_add_fusion.1
  29.4 0.0 copy-done.3
  29.5 0.1 add.359
  29.5 0.1 add.360
  29.6 0.1 iota_add_fusion
  29.8 0.1 broadcast_add_fusion
  29.9 0.1 fusion.15
  30.1 0.1 reshape.406
  30.2 116.1 %all-to-all-done = bf16[16,64,2880]{2,1,0:T(8,128)(2,1)} async-done(((bf16[16,64,2880]{2,1,0:T(8,128)(2,1)}), bf16[16,64,2880]{2,1,0:T(8,128)(2,1)}, u32[]{:S(2)}, u32[]{:S(2)}) %all-to-all-start) | async-done | bytes 5898272 | tf_op jit(solution)/shard_map/all_to_all | solution.py:104
  146.3 8.4 %fusion = f32[1024,768]{1,0:T(8,128)S(1)} fusion(bf16[1024,2880]{1,0:T(8,128)(2,1)} %bitcast.8, bf16[1,2880,768]{2,1,0:T(8,128)(2,1)} %param.13), kind=kOutput, calls=%fused_computation.4 | convolution fusion | flops 4529848320 | bytes 13467648 | tf_op jit(solution)/shard_map/dot_general | solution.py:59
  154.7 8.4 %fusion.2 = f32[1024,768]{1,0:T(8,128)S(1)} fusion(bf16[1024,2880]{1,0:T(8,128)(2,1)} %bitcast.8, bf16[1,2880,768]{2,1,0:T(8,128)(2,1)} %param.12), kind=kOutput, calls=%fused_computation.6 | convolution fusion | flops 4529848320 | bytes 13467648 | tf_op jit(solution)/shard_map/dot_general | solution.py:57
  163.1 4.4 %fusion.23 = f32[1024,16]{0,1:T(8,128)S(1)} fusion(bf16[1024,2880]{1,0:T(8,128)(2,1)} %bitcast.8, bf16[2880,8]{0,1:T(8,128)(2,1)S(1)} %get-tuple-element.10, bf16[2880,8]{0,1:T(8,128)(2,1)S(1)} %get-tuple-element.9), kind=kOutput, calls=%fused_computation.33 | convolution fusion | flops 94556160 | bytes 6055936 | tf_op jit(solution)/shard_map/dot_general | solution.py:40
  167.5 2.8 %fusion.27 = f32[1024,768]{1,0:T(8,128)S(1)} fusion(f32[1024,8]{0,1:T(8,128)S(1)} %reshape.403, f32[1024,16]{0,1:T(8,128)S(1)} %fusion.23, s32[768,8]{0,1:T(8,128)S(1)} %add.394, s32[8]{0:T(128)S(1)} %add.360), kind=kOutput, calls=%fused_computation.43 | convolution fusion | flops 75573248 | bytes 3236352 | tf_op jit(solution)/shard_map/dot_general | solution.py:46
  170.3 5.0 %multiply_convert_fusion = bf16[1024,768]{1,0:T(8,128)(2,1)} fusion(f32[1024,768]{1,0:T(8,128)S(1)} %fusion, f32[1024,768]{1,0:T(8,128)S(1)} %fusion.2, f32[1024,768]{1,0:T(8,128)S(1)} %fusion.27, f32[1024,8]{0,1:T(8,128)S(1)} %reshape.403, f32[1024,16]{0,1:T(8,128)S(1)} %fusion.23, s32[768,8]{0,1:T(8,128)S(1)} %add.404, s32[8]{0:T(128)S(1)} %add.360), kind=kOutput, calls=%fused_computation.8 | convolution fusion | flops 85010432 | bytes 11100672 | tf_op jit(solution)/shard_map/dot_general | solution.py:51
  175.3 0.0 copy-start.2
  175.3 0.0 copy-start.4
  175.3 0.0 copy-start.1
  175.3 19.8 %all-to-all-start.2 = ((bf16[16,64,768]{2,1,0:T(8,128)(2,1)}), bf16[16,64,768]{2,1,0:T(8,128)(2,1)S(1)}, u32[]{:S(2)}, u32[]{:S(2)}) async-start(bf16[16,64,768]{2,1,0:T(8,128)(2,1)} %bitcast.11), calls=%async_computation.2 | async-start | bytes 3145728 | tf_op jit(solution)/shard_map/all_to_all | solution.py:119
  195.1 0.1 compare_select_fusion
  195.2 0.1 reshape.418
  195.4 0.0 copy-done.2
  195.4 0.0 copy-done.4
  195.4 0.2 convolution_add_fusion
  195.6 0.0 copy-done.1
  195.7 0.1 copy.22
  195.8 32.6 %all-to-all-done.2 = bf16[16,64,768]{2,1,0:T(8,128)(2,1)S(1)} async-done(((bf16[16,64,768]{2,1,0:T(8,128)(2,1)}), bf16[16,64,768]{2,1,0:T(8,128)(2,1)S(1)}, u32[]{:S(2)}, u32[]{:S(2)}) %all-to-all-start.2) | async-done | bytes 1572896 | tf_op jit(solution)/shard_map/all_to_all | solution.py:119
  228.4 2.0 gather_fusion.1
  230.5 0.8 reshape.407
  231.2 1.5 multiply_convert_fusion.1
  (31 shorter events, 0.4 us)
Async XLA Ops:
  0.0 13.2 %copy-start = (bf16[64,2880]{1,0:T(8,128)(2,1)S(1)}, bf16[64,2880]{1,0:T(8,128)(2,1)}, u32[]{:S(2)}) copy-start(bf16[64,2880]{1,0:T(8,128)(2,1)} %param.7) | copy-start | bytes 1105924
  6.5 16.7 %all-to-all-start.1 = ((bf16[16,1,64]{2,1,0:T(2,128)(2,1)}), bf16[16,1,64]{2,1,0:T(2,128)(2,1)S(1)}, u32[]{:S(2)}, u32[]{:S(2)}) async-start(bf16[16,1,64]{2,1,0:T(2,128)(2,1)} %all_to_all.16), calls=%async_computation.1 | async-start | bytes 16384 | tf_op jit(solution)/shard_map/all_to_all | solution.py:105
  23.2 6.3 %copy-start.3 = (s32[2]{0:T(128)S(1)}, s32[2]{0:T(128)}, u32[]{:S(2)}) copy-start(s32[2]{0:T(128)} %param.11) | copy-start | bytes 28
  23.2 123.2 %all-to-all-start = ((bf16[16,64,2880]{2,1,0:T(8,128)(2,1)}), bf16[16,64,2880]{2,1,0:T(8,128)(2,1)}, u32[]{:S(2)}, u32[]{:S(2)}) async-start(bf16[16,64,2880]{2,1,0:T(8,128)(2,1)} %bitcast.39), calls=%async_computation | async-start | bytes 12058624 | tf_op jit(solution)/shard_map/all_to_all | solution.py:104
  175.3 20.1 %copy-start.2 = (bf16[2880,8]{0,1:T(8,128)(2,1)S(1)}, bf16[2880,8]{0,1:T(8,128)(2,1)}, u32[]{:S(2)}) copy-start(bf16[2880,8]{0,1:T(8,128)(2,1)} %param.9) | copy-start | bytes 138244
  175.3 20.1 %copy-start.4 = (f32[8]{0:T(128)S(1)}, f32[8]{0:T(128)}, u32[]{:S(2)}) copy-start(f32[8]{0:T(128)} %param.10) | copy-start | bytes 100
  175.3 20.3 %copy-start.1 = (s32[64,4]{0,1:T(4,128)S(1)}, s32[64,4]{0,1:T(4,128)}, u32[]{:S(2)}) copy-start(s32[64,4]{0,1:T(4,128)} %param.8) | copy-start | bytes 3076
  175.3 53.2 %all-to-all-start.2 = ((bf16[16,64,768]{2,1,0:T(8,128)(2,1)}), bf16[16,64,768]{2,1,0:T(8,128)(2,1)S(1)}, u32[]{:S(2)}, u32[]{:S(2)}) async-start(bf16[16,64,768]{2,1,0:T(8,128)(2,1)} %bitcast.11), calls=%async_computation.2 | async-start | bytes 3145728 | tf_op jit(solution)/shard_map/all_to_all | solution.py:119
where the time goes:
time: 236 us; the launch traced here: 233 us
  waiting for transfers between devices  149 us (63%)
  starting transfers between devices  32.6 us (14%)
  matrix products  29.1 us (12%)
  other arithmetic  11.3 us (5%)
  local copies, waits for them, and re-layouts  10.7 us (5%)
    all_to_all x1, waiting for transfers between devices, local(): lax.all_to_all(send_rows, 'exp', split_axis=0, concat_axis=0, tiled=True)  116 us
    all_to_all x1, waiting for transfers between devices, local(): lax.all_to_all(activation, 'exp', split_axis=0, concat_axis=0, tiled=True)  32.6 us
    all_to_all x1, starting transfers between devices, local(): lax.all_to_all(activation, 'exp', split_axis=0, concat_axis=0, tiled=True)  19.8 us
    dot_general x1, matrix products, expert_rows(): jnp.dot(inputs, gate_cols, preferred_element_type=jnp.float32)  8.4 us
    dot_general x1, matrix products, expert_rows(): jnp.dot(inputs, up_cols, preferred_element_type=jnp.float32)  8.39 us
    scatter x1, other arithmetic, local(): jnp.zeros((device_count * capacity, feature_width), jnp.bfloat16).at[target]  8.32 us
    all_to_all x1, starting transfers between devices, local(): lax.all_to_all(send_labels, 'exp', split_axis=0, concat_axis=0, tiled=True)  6.67 us
    all_to_all x1, starting transfers between devices, local(): lax.all_to_all(send_rows, 'exp', split_axis=0, concat_axis=0, tiled=True)  6.15 us
  transfers between devices with their start and end apart: 3, of which 2 were waited for; matrix products, arithmetic and copies ran while one was open for 5% of the time, Pallas kernels for 0%

commit v1 on v0

--- a/solution.py
+++ b/solution.py
@@ -1,8 +1,11 @@
+import functools
 import math
 
 import jax
 import jax.numpy as jnp
 from jax import lax
+from jax.experimental import pallas as pl
+from jax.experimental.pallas import tpu as pltpu
 from jax.sharding import PartitionSpec as P
 
 FW = 1536
@@ -126,6 +129,315 @@
     return routed.reshape(tok_rows, top_count, 2, quarter)
 
 
+Z, X, C = 4, 2, 2
+ROW = X * C
+MESH = pl.DeviceIdType.MESH
+
+
+def levels(seeds, counter):
+    hashed = (seeds * 31 + counter) * 1103515245 + 12345
+    hashed = hashed ^ (hashed >> 16)
+    hashed = hashed * 747796405
+    return (((hashed >> 16) & 255) - 128).astype(jnp.float32) / 128.0
+
+
+def row_seeds(seed_ref, member, members):
+    seeds = jnp.zeros_like(member)
+    for index in range(members):
+        seeds = jnp.where(member == index, seed_ref[index], seeds)
+    return seeds
+
+
+def fused(
+    expert_count, seed_ref, tokens, routes, router, bias, gate, up, out,
+    held, wg, wu, gt, ut, left, act, back, gsend, grecv, rsend, rrecv, wsem,
+):
+    count = Z * ROW
+    rows, width = held.shape[1:]
+    hidden = wg.shape[1]
+    members = seed_ref.shape[0]
+    me = lax.axis_index("exp")
+    z, x, c = me // ROW, (me // C) % X, me % C
+    expert, half = me // 2, me % 2
+    whole = width // 128 * 128
+    rest = width - whole
+    beside, sibling = me + C * (1 - 2 * x), me + 1 - 2 * c
+
+    load = pltpu.make_async_copy(tokens, held.at[me], wsem.at[0])
+    load.start()
+    load_g = pltpu.make_async_copy(gate.at[0], wg, wsem.at[1])
+    load_g.start()
+    load_u = pltpu.make_async_copy(up.at[0], wu, wsem.at[2])
+    load_u.start()
+
+    barrier = pltpu.get_barrier_semaphore()
+
+    def greet(k, carry):
+        pl.semaphore_signal(
+            barrier, inc=1, device_id={"exp": (me + k) % count}, device_id_type=MESH
+        )
+        return carry
+
+    lax.fori_loop(1, count, greet, 0)
+    load.wait()
+    pl.semaphore_wait(barrier, count - 1)
+
+    def pass_on(slot, way, target):
+        return pltpu.make_async_remote_copy(
+            src_ref=held.at[slot], dst_ref=held.at[slot],
+            send_sem=gsend.at[slot, way], recv_sem=grecv.at[slot],
+            device_id={"exp": target}, device_id_type=MESH,
+        )
+
+    def arrived(slot):
+        pass_on(slot, 3, sibling).wait_recv()
+
+    def give_back(slot):
+        return pltpu.make_async_remote_copy(
+            src_ref=act.at[slot], dst_ref=back.at[half, expert],
+            send_sem=rsend.at[slot], recv_sem=rrecv.at[me],
+            device_id={"exp": slot}, device_id_type=MESH,
+        )
+
+    @pl.when(z < Z - 1)
+    def _():
+        pass_on(me, 0, me + ROW).start()
+
+    @pl.when(z > 0)
+    def _():
+        pass_on(me, 1, me - ROW).start()
+
+    pass_on(me, 2, beside).start()
+    pass_on(me, 3, sibling).start()
+
+    noisy = 8 * members
+    k = lax.broadcasted_iota(jnp.int32, (noisy, width), 0)
+    i = lax.broadcasted_iota(jnp.int32, (noisy, width), 1)
+    seeds = row_seeds(seed_ref, (k // 4) % members, members)
+    number = ((k // (4 * members)) * expert_count + expert) * 4 + k % 4
+    left[...] = levels(seeds, number * 4096 + i).astype(jnp.bfloat16)
+    k = lax.broadcasted_iota(jnp.int32, (noisy, hidden), 0)
+    i = lax.broadcasted_iota(jnp.int32, (noisy, hidden), 1) + half * hidden
+    seeds = row_seeds(seed_ref, (k // 4) % members, members)
+    number = ((2 + k // (4 * members)) * expert_count + expert) * 4 + k % 4
+    right = levels(seeds, number * 4096 + i)
+    for ref, tag in ((gt, 0), (ut, 1)):
+        part = jnp.where(k // (4 * members) == tag, right, 0.0).astype(jnp.bfloat16)
+        ref[rest:, :] = jnp.zeros((ref.shape[0] - rest, hidden), jnp.bfloat16)
+        for piece in range(3):
+            ref[rest + piece * noisy : rest + (piece + 1) * noisy, :] = part
+    top = routes.shape[1]
+    logits = jnp.dot(held[me], router[...], preferred_element_type=jnp.float32) + bias[...]
+    ids = lax.broadcasted_iota(jnp.int32, logits.shape, 1)
+    chosen = [
+        jnp.sum(jnp.where(routes[:, j : j + 1] == ids, logits, 0.0), axis=1, keepdims=True)
+        for j in range(top)
+    ]
+    peak = functools.reduce(jnp.maximum, chosen)
+    grown = [jnp.exp(v - peak) for v in chosen]
+    total = sum(grown[1:], grown[0])
+    weights = jnp.concatenate([v / total for v in grown], axis=0)
+    place = lax.broadcasted_iota(jnp.int32, (rows, expert_count * rows), 1)
+    token = lax.broadcasted_iota(jnp.int32, (rows, expert_count * rows), 0)
+    pick = jnp.concatenate(
+        [
+            jnp.where(place == routes[:, j : j + 1] * rows + token, 1.0, 0.0).astype(jnp.bfloat16)
+            for j in range(top)
+        ],
+        axis=0,
+    )
+
+    load_g.wait()
+    load_u.wait()
+    gt[0:rest, :] = wg[whole:, :]
+    ut[0:rest, :] = wu[whole:, :]
+
+    scale = NOISE / math.sqrt(width)
+    batch = ROW * rows
+    tile = 256
+
+    def visit(step, carry):
+        above = step + 1
+
+        @pl.when(z - above >= 0)
+        def _():
+            slot = me - above * ROW
+            arrived(slot)
+
+            @pl.when(z < Z - 1)
+            def _():
+                pass_on(slot, 0, me + ROW).start()
+
+            pass_on(slot, 2, beside).start()
+            pass_on(slot, 3, sibling).start()
+
+        @pl.when(z + above < Z)
+        def _():
+            slot = me + above * ROW
+            arrived(slot)
+
+            @pl.when(z > 0)
+            def _():
+                pass_on(slot, 1, me - ROW).start()
+
+            pass_on(slot, 2, beside).start()
+            pass_on(slot, 3, sibling).start()
+
+        mirror = z // 2
+        folded = z + mirror * (3 - 2 * z)
+        first = 1 - step // 2
+        near = first * (folded + (step % 2) * (1 - 2 * folded)) + (1 - first) * step
+        row = near + mirror * (3 - 2 * near)
+        base = row * ROW
+        across = base + (1 - x) * C + c
+        arrived(across)
+        pass_on(across, 3, sibling).start()
+
+        @pl.when(step == 0)
+        def _():
+            arrived(sibling)
+
+        @pl.when(step > 0)
+        def _():
+            arrived(base + x * C + 1 - c)
+
+        arrived(base + (1 - x) * C + 1 - c)
+
+        values = held[pl.ds(base, ROW)].reshape(batch, width)
+        projected = lax.dot_general(
+            values, left[...], (((1,), (1,)), ((), ())), preferred_element_type=jnp.float32
+        )
+        where = base * rows + lax.broadcasted_iota(jnp.int32, (batch, noisy), 0)
+        member = (lax.broadcasted_iota(jnp.int32, (batch, noisy), 1) // 4) % members
+        remaining = jnp.where(where // LENGTH == member, projected * scale, 0.0)
+        ends = [values[:, whole:]]
+        for _ in range(3):
+            piece = remaining.astype(jnp.bfloat16)
+            remaining = remaining - piece.astype(jnp.float32)
+            ends.append(piece)
+        ends.append(jnp.zeros((batch, 128 - rest - 3 * noisy), jnp.bfloat16))
+        end = jnp.concatenate(ends, axis=1)
+
+        def columns(n, carry):
+            at = pl.ds(pl.multiple_of(n * tile, tile), tile)
+            start = held[pl.ds(base, ROW), :, 0:whole].reshape(batch, whole)
+            g = jnp.dot(start, wg[0:whole, at], preferred_element_type=jnp.float32)
+            g = g + jnp.dot(end, gt[:, at], preferred_element_type=jnp.float32)
+            u = jnp.dot(start, wu[0:whole, at], preferred_element_type=jnp.float32)
+            u = u + jnp.dot(end, ut[:, at], preferred_element_type=jnp.float32)
+            value = (g * jax.nn.sigmoid(ALPHA * g) * (u + 1.0)).astype(jnp.bfloat16)
+            act[pl.ds(base, ROW), :, at] = value.reshape(ROW, rows, tile)
+            return carry
+
+        lax.fori_loop(0, hidden // tile, columns, 0)
+        for other in range(ROW):
+            @pl.when(base + other != me)
+            def _(slot=base + other):
+                give_back(slot).start()
+        return carry
+
+    lax.fori_loop(0, Z, visit, 0)
+    back[half, expert] = act[me]
+
+    def take(k, carry):
+        slot = (me + k) % count
+        pltpu.make_async_remote_copy(
+            src_ref=act.at[slot], dst_ref=back.at[slot % 2, slot // 2],
+            send_sem=rsend.at[slot], recv_sem=rrecv.at[slot],
+            device_id={"exp": slot}, device_id_type=MESH,
+        ).wait_recv()
+        return carry
+
+    lax.fori_loop(1, count, take, 0)
+    for h in range(2):
+        found = jnp.dot(
+            pick, back[h].reshape(expert_count * rows, hidden), preferred_element_type=jnp.float32
+        )
+        out[:, h * hidden : (h + 1) * hidden] = (found * weights).astype(jnp.bfloat16)
+
+    def sent(k, carry):
+        slot = (me + k) % count
+        give_back(slot).wait_send()
+        return carry
+
+    lax.fori_loop(1, count, sent, 0)
+
+    def passed(zo, carry):
+        slot = zo * ROW + x * C + c
+
+        @pl.when((zo <= z) & (z < Z - 1))
+        def _():
+            pass_on(slot, 0, me + ROW).wait_send()
+
+        @pl.when((zo >= z) & (z > 0))
+        def _():
+            pass_on(slot, 1, me - ROW).wait_send()
+
+        pass_on(slot, 2, beside).wait_send()
+        pass_on(slot, 3, sibling).wait_send()
+        pass_on(zo * ROW + (1 - x) * C + c, 3, sibling).wait_send()
+        return carry
+
+    lax.fori_loop(0, Z, passed, 0)
+
+
+def gathered(tokens, routes, router_weight, router_bias, member_seeds, gate_weight, up_weight):
+    rows, width = tokens.shape
+    top = routes.shape[1]
+    expert_count = router_weight.shape[1]
+    hidden = gate_weight.shape[2]
+    count = Z * ROW
+    noisy = 8 * member_seeds.shape[0]
+    vmem = pl.BlockSpec(memory_space=pltpu.VMEM)
+    anywhere = pl.BlockSpec(memory_space=pl.ANY)
+    half_dtype = jnp.bfloat16
+    result = pl.pallas_call(
+        functools.partial(fused, expert_count),
+        out_shape=jax.ShapeDtypeStruct((top * rows, 2 * hidden), half_dtype),
+        in_specs=[
+            pl.BlockSpec(memory_space=pltpu.SMEM), anywhere, vmem, vmem, vmem, anywhere, anywhere,
+        ],
+        out_specs=vmem,
+        scratch_shapes=[
+            pltpu.VMEM((count, rows, width), half_dtype),
+            pltpu.VMEM((width, hidden), half_dtype),
+            pltpu.VMEM((width, hidden), half_dtype),
+            pltpu.VMEM((128, hidden), half_dtype),
+            pltpu.VMEM((128, hidden), half_dtype),
+            pltpu.VMEM((noisy, width), half_dtype),
+            pltpu.VMEM((count, rows, hidden), half_dtype),
+            pltpu.VMEM((2, expert_count, rows, hidden), half_dtype),
+            pltpu.SemaphoreType.DMA((count, 4)),
+            pltpu.SemaphoreType.DMA((count,)),
+            pltpu.SemaphoreType.DMA((count,)),
+            pltpu.SemaphoreType.DMA((count,)),
+            pltpu.SemaphoreType.DMA((3,)),
+        ],
+        compiler_params=pltpu.CompilerParams(
+            collective_id=0, has_side_effects=True, vmem_limit_bytes=48 * 1024 * 1024
+        ),
+        cost_estimate=pl.CostEstimate(
+            flops=4 * count * rows * width * hidden,
+            bytes_accessed=4 * width * hidden,
+            transcendentals=count * rows * hidden,
+        ),
+    )(member_seeds, tokens, routes, router_weight, router_bias[None, :], gate_weight, up_weight)
+    return result.reshape(top, rows, 2, hidden).transpose(1, 0, 2, 3)
+
+
+def fits(mesh, tokens, routes, router_weight, member_seeds, gate_weight):
+    devices = mesh.shape["exp"]
+    rows = tokens.shape[0] // (mesh.shape["pop"] * devices)
+    experts = router_weight.shape[1]
+    return (
+        mesh.shape["tp"] == 1
+        and devices == Z * ROW == 2 * experts
+        and 2 * rows * routes.shape[1] // experts >= rows
+        and tokens.shape[1] % 128 + 24 * (member_seeds.shape[0] // mesh.shape["pop"]) <= 128
+        and gate_weight.shape[2] % 256 == 0
+    )
+
+
 def solution(mesh):
     in_specs = (
         P(("pop", "exp"), "tp"),
@@ -137,4 +449,12 @@
         P("exp", None, "tp"),
     )
     out_specs = P(("pop", "exp"), None, None, "tp")
-    return jax.shard_map(local, mesh=mesh, in_specs=in_specs, out_specs=out_specs, check_vma=False)
+
+    def whole(tokens, routes, router_weight, router_bias, member_seeds, gate_weight, up_weight):
+        small = fits(mesh, tokens, routes, router_weight, member_seeds, gate_weight)
+        body = gathered if small else local
+        return jax.shard_map(
+            body, mesh=mesh, in_specs=in_specs, out_specs=out_specs, check_vma=False
+        )(tokens, routes, router_weight, router_bias, member_seeds, gate_weight, up_weight)
+
+    return whole

time: 236 us -> 85.9 us (0.36); the launches traced: 233 us -> 85.7 us
  waiting for transfers between devices: 149 us -> 0 us
  Pallas kernels: 0 us -> 79.8 us
  starting transfers between devices: 32.6 us -> 0 us
  matrix products: 29.1 us -> 0 us
  other arithmetic: 11.3 us -> 0 us
  local copies, waits for them, and re-layouts: 10.7 us -> 5.89 us
    all_to_all x3 -> x0, waiting for transfers between devices: 149 us -> none  [the longest x1 116 us: local(): lax.all_to_all(send_rows, 'exp', split_axis=0, concat_axis=0, tiled=True)]
    pallas_call x0 -> x1, Pallas kernels: none -> 79.8 us  [gathered(): pl.pallas_call(functools.partial(fused, expert_count), out_shape=jax.Shap...]
    all_to_all x3 -> x0, starting transfers between devices: 32.6 us -> none  [the longest x1 19.8 us: local(): lax.all_to_all(activation, 'exp', split_axis=0, concat_axis=0, tiled=True)]
    dot_general x6 -> x0, matrix products: 29.1 us -> none  [the longest x1 8.4 us: expert_rows(): jnp.dot(inputs, gate_cols, preferred_element_type=jnp.float32)]
    scatter x1 -> x0, other arithmetic: 8.32 us -> none  [local(): jnp.zeros((device_count * capacity, feature_width), jnp.bfloat16).at[target]]
    scatter x1 -> x0, local copies, waits for them, and re-layouts: 3.77 us -> none  [local(): jnp.full((device_count * capacity,), -1.0, jnp.bfloat16).at[target]]
    gather x2 -> x0, local copies, waits for them, and re-layouts: 3.64 us -> none  [the longest x1 2.02 us: local(): picked = returned[pick_index]]
    unnamed x11 -> x8, local copies, waits for them, and re-layouts: 0.84 us -> 4.29 us
  transfers between devices with their start and end apart: 3 -> 0, of which waited for: 2 -> 0; matrix products, arithmetic and copies ran while one was open for 5% -> 0% of each run, Pallas kernels for 0% -> 0%
where the time goes in v1:
time: 85.9 us; the launch traced here: 85.7 us
  Pallas kernels  79.8 us (93%)
  local copies, waits for them, and re-layouts  5.89 us (7%)
    pallas_call x1, Pallas kernels, gathered(): pl.pallas_call(functools.partial(fused, expert_count), out_shape=jax.Shap...  79.8 us
    unnamed x8, local copies, waits for them, and re-layouts  4.29 us

profile of v1, /device:TPU:3, one launch (start us, length us, event | category | flops | bytes accessed | tf_op | source)
XLA Modules:
  0.0 85.7 jit_solution(12793716252467566744)
XLA Ops:
  0.0 0.8 copy.8.routes
  0.8 1.2 %copy.9.router = bf16[2880,8]{1,0:T(8,128)(2,1)S(1)} copy(bf16[2880,8]{0,1:T(8,128)(2,1)} %param.9) | data formatting | bytes 92160 | tf_op args[2]
  2.0 0.0 copy-start
  2.0 1.0 %copy-done = bf16[64,2880]{1,0:T(8,128)(2,1)S(1)} copy-done((bf16[64,2880]{1,0:T(8,128)(2,1)S(1)}, bf16[64,2880]{1,0:T(8,128)(2,1)}, u32[]{:S(2)}) %copy-start) | copy-done | bytes 368664
  3.0 0.0 copy-start.1
  3.0 0.7 copy-done.1
  3.7 0.0 copy-start.2
  3.7 0.7 copy-done.2
  4.3 79.8 %shard_map.73 = bf16[256,1536]{1,0:T(8,128)(2,1)S(1)} custom-call(s32[2]{0:T(128)S(1)} %copy-done.1, bf16[64,2880]{1,0:T(8,128)(2,1)S(1)} %copy-done, s32[64,4]{1,0:T(8,128)S(1)} %copy.8.routes, bf16[2880,8]{1,0:T(8,128)(2,1)S(1)} %copy.9.router, f32[1,8]{1,0:T(1,128)S(1)} %bitcast.4, bf16[1,2880,768]{2,1,0:T(8,128)(2,1)} %gate.1, bf16[1,2880,768]{2,1,0:T(8,128)(2,1)} %up.1), custom_call_target="tpu_custom_call" | custom-call | flops 9059696640 | bytes 8847360 | tf_op jit(solution)/shard_map/pallas_call | solution.py:394
  84.1 0.2 reshape.3
  84.3 1.4 %copy.12 = bf16[4,64,2,768]{3,2,0,1:T(2,128)(2,1)} copy(bf16[4,64,2,768]{3,2,1,0:T(2,128)(2,1)S(1)} %reshape.3) | data formatting | bytes 1572864 | tf_op jit(solution)/shard_map/reshape | solution.py:425
Async XLA Ops:
  2.0 1.0 %copy-start = (bf16[64,2880]{1,0:T(8,128)(2,1)S(1)}, bf16[64,2880]{1,0:T(8,128)(2,1)}, u32[]{:S(2)}) copy-start(bf16[64,2880]{1,0:T(8,128)(2,1)} %tokens.1) | copy-start | bytes 1105924
  3.0 0.7 copy-start.1
  3.7 0.7 copy-start.2

commit v2 on v1

--- a/solution.py
+++ b/solution.py
@@ -149,7 +149,8 @@
 
 
 def fused(
-    expert_count, seed_ref, tokens, routes, router, bias, gate, up, out,
+    expert_count, seed_hbm, tokens, routes_hbm, router, bias_hbm, gate, up, out,
+    seed_ref, routes, bias,
     held, wg, wu, gt, ut, left, act, back, gsend, grecv, rsend, rrecv, wsem,
 ):
     count = Z * ROW
@@ -165,6 +166,14 @@
 
     load = pltpu.make_async_copy(tokens, held.at[me], wsem.at[0])
     load.start()
+    small = [
+        pltpu.make_async_copy(source, target, wsem.at[3 + index])
+        for index, (source, target) in enumerate(
+            [(seed_hbm, seed_ref), (routes_hbm, routes), (bias_hbm, bias)]
+        )
+    ]
+    for copy in small:
+        copy.start()
     load_g = pltpu.make_async_copy(gate.at[0], wg, wsem.at[1])
     load_g.start()
     load_u = pltpu.make_async_copy(up.at[0], wu, wsem.at[2])
@@ -182,15 +191,18 @@
     load.wait()
     pl.semaphore_wait(barrier, count - 1)
 
-    def pass_on(slot, way, target):
+    cut = rows // 2
+
+    def pass_on(slot, piece, way, target):
+        block = held.at[slot, pl.ds(piece * cut, cut)]
         return pltpu.make_async_remote_copy(
-            src_ref=held.at[slot], dst_ref=held.at[slot],
-            send_sem=gsend.at[slot, way], recv_sem=grecv.at[slot],
+            src_ref=block, dst_ref=block,
+            send_sem=gsend.at[slot, piece, way], recv_sem=grecv.at[slot, piece],
             device_id={"exp": target}, device_id_type=MESH,
         )
 
-    def arrived(slot):
-        pass_on(slot, 3, sibling).wait_recv()
+    def arrived(slot, piece):
+        pass_on(slot, piece, 3, sibling).wait_recv()
 
     def give_back(slot):
         return pltpu.make_async_remote_copy(
@@ -199,17 +211,70 @@
             device_id={"exp": slot}, device_id_type=MESH,
         )
 
-    @pl.when(z < Z - 1)
-    def _():
-        pass_on(me, 0, me + ROW).start()
-
-    @pl.when(z > 0)
-    def _():
-        pass_on(me, 1, me - ROW).start()
-
-    pass_on(me, 2, beside).start()
-    pass_on(me, 3, sibling).start()
-
+    for piece in range(2):
+        @pl.when(z < Z - 1)
+        def _(piece=piece):
+            pass_on(me, piece, 0, me + ROW).start()
+
+        @pl.when(z > 0)
+        def _(piece=piece):
+            pass_on(me, piece, 1, me - ROW).start()
+
+        pass_on(me, piece, 2, beside).start()
+        pass_on(me, piece, 3, sibling).start()
+
+    def chip_row(step):
+        mirror = z // 2
+        near = (z + mirror * (3 - 2 * z) + step) % Z
+        return near + mirror * (3 - 2 * near)
+
+    def relay(step, piece):
+        above = step + 1
+
+        @pl.when(z - above >= 0)
+        def _():
+            slot = me - above * ROW
+            arrived(slot, piece)
+
+            @pl.when(z < Z - 1)
+            def _():
+                pass_on(slot, piece, 0, me + ROW).start()
+
+            @pl.when(z != 1)
+            def _():
+                pass_on(slot, piece, 2, beside).start()
+
+            pass_on(slot, piece, 3, sibling).start()
+
+        @pl.when(z + above < Z)
+        def _():
+            slot = me + above * ROW
+            arrived(slot, piece)
+
+            @pl.when(z > 0)
+            def _():
+                pass_on(slot, piece, 1, me - ROW).start()
+
+            @pl.when(z != Z - 2)
+            def _():
+                pass_on(slot, piece, 2, beside).start()
+
+            pass_on(slot, piece, 3, sibling).start()
+
+        @pl.when((above == 2) & (z == 1))
+        def _():
+            pass_on(me - ROW, piece, 2, beside).start()
+
+        @pl.when((above == 2) & (z == Z - 2))
+        def _():
+            pass_on(me + ROW, piece, 2, beside).start()
+
+        across = chip_row(step) * ROW + (1 - x) * C + c
+        arrived(across, piece)
+        pass_on(across, piece, 3, sibling).start()
+
+    for copy in small:
+        copy.wait()
     noisy = 8 * members
     k = lax.broadcasted_iota(jnp.int32, (noisy, width), 0)
     i = lax.broadcasted_iota(jnp.int32, (noisy, width), 1)
@@ -226,27 +291,7 @@
         ref[rest:, :] = jnp.zeros((ref.shape[0] - rest, hidden), jnp.bfloat16)
         for piece in range(3):
             ref[rest + piece * noisy : rest + (piece + 1) * noisy, :] = part
-    top = routes.shape[1]
-    logits = jnp.dot(held[me], router[...], preferred_element_type=jnp.float32) + bias[...]
-    ids = lax.broadcasted_iota(jnp.int32, logits.shape, 1)
-    chosen = [
-        jnp.sum(jnp.where(routes[:, j : j + 1] == ids, logits, 0.0), axis=1, keepdims=True)
-        for j in range(top)
-    ]
-    peak = functools.reduce(jnp.maximum, chosen)
-    grown = [jnp.exp(v - peak) for v in chosen]
-    total = sum(grown[1:], grown[0])
-    weights = jnp.concatenate([v / total for v in grown], axis=0)
-    place = lax.broadcasted_iota(jnp.int32, (rows, expert_count * rows), 1)
-    token = lax.broadcasted_iota(jnp.int32, (rows, expert_count * rows), 0)
-    pick = jnp.concatenate(
-        [
-            jnp.where(place == routes[:, j : j + 1] * rows + token, 1.0, 0.0).astype(jnp.bfloat16)
-            for j in range(top)
-        ],
-        axis=0,
-    )
-
+    relay(0, 0)
     load_g.wait()
     load_u.wait()
     gt[0:rest, :] = wg[whole:, :]
@@ -257,52 +302,15 @@
     tile = 256
 
     def visit(step, carry):
-        above = step + 1
-
-        @pl.when(z - above >= 0)
-        def _():
-            slot = me - above * ROW
-            arrived(slot)
-
-            @pl.when(z < Z - 1)
-            def _():
-                pass_on(slot, 0, me + ROW).start()
-
-            pass_on(slot, 2, beside).start()
-            pass_on(slot, 3, sibling).start()
-
-        @pl.when(z + above < Z)
-        def _():
-            slot = me + above * ROW
-            arrived(slot)
-
-            @pl.when(z > 0)
-            def _():
-                pass_on(slot, 1, me - ROW).start()
-
-            pass_on(slot, 2, beside).start()
-            pass_on(slot, 3, sibling).start()
-
-        mirror = z // 2
-        folded = z + mirror * (3 - 2 * z)
-        first = 1 - step // 2
-        near = first * (folded + (step % 2) * (1 - 2 * folded)) + (1 - first) * step
-        row = near + mirror * (3 - 2 * near)
-        base = row * ROW
-        across = base + (1 - x) * C + c
-        arrived(across)
-        pass_on(across, 3, sibling).start()
-
-        @pl.when(step == 0)
-        def _():
-            arrived(sibling)
-
         @pl.when(step > 0)
         def _():
-            arrived(base + x * C + 1 - c)
-
-        arrived(base + (1 - x) * C + 1 - c)
-
+            relay(step, 0)
+
+        relay(step, 1)
+        base = chip_row(step) * ROW
+        for piece in range(2):
+            arrived(base + x * C + 1 - c, piece)
+            arrived(base + (1 - x) * C + 1 - c, piece)
         values = held[pl.ds(base, ROW)].reshape(batch, width)
         projected = lax.dot_general(
             values, left[...], (((1,), (1,)), ((), ())), preferred_element_type=jnp.float32
@@ -330,14 +338,48 @@
             return carry
 
         lax.fori_loop(0, hidden // tile, columns, 0)
-        for other in range(ROW):
-            @pl.when(base + other != me)
-            def _(slot=base + other):
-                give_back(slot).start()
+
+        @pl.when(step > 0)
+        def _():
+            for other in range(ROW):
+                give_back(base + other).start()
         return carry
 
     lax.fori_loop(0, Z, visit, 0)
+    give_back(beside).start()
+    give_back(beside + 1 - 2 * c).start()
+    give_back(sibling).start()
     back[half, expert] = act[me]
+
+    top = routes.shape[0]
+    logits = lax.dot_general(
+        held[me], router[...], (((1,), (1,)), ((), ())), preferred_element_type=jnp.float32
+    )
+    logits = logits + bias[...]
+    ids = lax.broadcasted_iota(jnp.int32, logits.shape, 1).astype(jnp.float32)
+    line = lax.broadcasted_iota(jnp.int32, (rows, rows), 0)
+    unit = jnp.where(line == lax.broadcasted_iota(jnp.int32, (rows, rows), 1), 1.0, 0.0)
+    named = lax.dot_general(
+        unit.astype(jnp.bfloat16), routes[...].astype(jnp.float32).astype(jnp.bfloat16),
+        (((1,), (1,)), ((), ())), preferred_element_type=jnp.float32,
+    )
+    chosen = [
+        jnp.sum(jnp.where(named[:, j : j + 1] == ids, logits, 0.0), axis=1, keepdims=True)
+        for j in range(top)
+    ]
+    peak = functools.reduce(jnp.maximum, chosen)
+    grown = [jnp.exp(v - peak) for v in chosen]
+    total = sum(grown[1:], grown[0])
+    weights = jnp.concatenate([v / total for v in grown], axis=0)
+    place = lax.broadcasted_iota(jnp.int32, (rows, expert_count * rows), 1).astype(jnp.float32)
+    token = lax.broadcasted_iota(jnp.int32, (rows, expert_count * rows), 0).astype(jnp.float32)
+    pick = jnp.concatenate(
+        [
+            jnp.where(place == named[:, j : j + 1] * rows + token, 1.0, 0.0).astype(jnp.bfloat16)
+            for j in range(top)
+        ],
+        axis=0,
+    )
 
     def take(k, carry):
         slot = (me + k) % count
@@ -362,23 +404,24 @@
 
     lax.fori_loop(1, count, sent, 0)
 
-    def passed(zo, carry):
+    def passed(k, carry):
+        zo, piece = k // 2, k % 2
         slot = zo * ROW + x * C + c
 
         @pl.when((zo <= z) & (z < Z - 1))
         def _():
-            pass_on(slot, 0, me + ROW).wait_send()
+            pass_on(slot, piece, 0, me + ROW).wait_send()
 
         @pl.when((zo >= z) & (z > 0))
         def _():
-            pass_on(slot, 1, me - ROW).wait_send()
-
-        pass_on(slot, 2, beside).wait_send()
-        pass_on(slot, 3, sibling).wait_send()
-        pass_on(zo * ROW + (1 - x) * C + c, 3, sibling).wait_send()
+            pass_on(slot, piece, 1, me - ROW).wait_send()
+
+        pass_on(slot, piece, 2, beside).wait_send()
+        pass_on(slot, piece, 3, sibling).wait_send()
+        pass_on(zo * ROW + (1 - x) * C + c, piece, 3, sibling).wait_send()
         return carry
 
-    lax.fori_loop(0, Z, passed, 0)
+    lax.fori_loop(0, 2 * Z, passed, 0)
 
 
 def gathered(tokens, routes, router_weight, router_bias, member_seeds, gate_weight, up_weight):
@@ -394,11 +437,12 @@
     result = pl.pallas_call(
         functools.partial(fused, expert_count),
         out_shape=jax.ShapeDtypeStruct((top * rows, 2 * hidden), half_dtype),
-        in_specs=[
-            pl.BlockSpec(memory_space=pltpu.SMEM), anywhere, vmem, vmem, vmem, anywhere, anywhere,
-        ],
+        in_specs=[anywhere] * 3 + [vmem] + [anywhere] * 3,
         out_specs=vmem,
         scratch_shapes=[
+            pltpu.SMEM(member_seeds.shape, jnp.int32),
+            pltpu.VMEM((top, rows), jnp.int32),
+            pltpu.VMEM((1, expert_count), jnp.float32),
             pltpu.VMEM((count, rows, width), half_dtype),
             pltpu.VMEM((width, hidden), half_dtype),
             pltpu.VMEM((width, hidden), half_dtype),
@@ -407,21 +451,23 @@
             pltpu.VMEM((noisy, width), half_dtype),
             pltpu.VMEM((count, rows, hidden), half_dtype),
             pltpu.VMEM((2, expert_count, rows, hidden), half_dtype),
-            pltpu.SemaphoreType.DMA((count, 4)),
+            pltpu.SemaphoreType.DMA((count, 2, 4)),
+            pltpu.SemaphoreType.DMA((count, 2)),
             pltpu.SemaphoreType.DMA((count,)),
             pltpu.SemaphoreType.DMA((count,)),
-            pltpu.SemaphoreType.DMA((count,)),
-            pltpu.SemaphoreType.DMA((3,)),
+            pltpu.SemaphoreType.DMA((6,)),
         ],
         compiler_params=pltpu.CompilerParams(
-            collective_id=0, has_side_effects=True, vmem_limit_bytes=48 * 1024 * 1024
+            collective_id=0, has_side_effects=True, vmem_limit_bytes=60 * 1024 * 1024
         ),
         cost_estimate=pl.CostEstimate(
             flops=4 * count * rows * width * hidden,
             bytes_accessed=4 * width * hidden,
             transcendentals=count * rows * hidden,
         ),
-    )(member_seeds, tokens, routes, router_weight, router_bias[None, :], gate_weight, up_weight)
+    )(
+        member_seeds, tokens, routes.T, router_weight.T, router_bias[None, :], gate_weight, up_weight
+    )
     return result.reshape(top, rows, 2, hidden).transpose(1, 0, 2, 3)
 
 

time: 85.9 us -> 83.2 us (0.969)
  local copies, waits for them, and re-layouts: 5.89 us -> 3.68 us
    unnamed x8 -> x0, local copies, waits for them, and re-layouts: 4.29 us -> none
    reshape x2, local copies, waits for them, and re-layouts: 1.6 us -> 3.68 us  [gathered(): return result.reshape(top, rows, 2, hidden).transpose(1, 0, 2, 3)]
where the time goes in v2:
time: 83.2 us; the launch traced here: 83 us
  Pallas kernels  79.3 us (95%)
  local copies, waits for them, and re-layouts  3.68 us (4%)
    pallas_call x1, Pallas kernels, gathered(): pl.pallas_call(functools.partial(fused, expert_count), out_shape=jax.Shap...  79.3 us
    reshape x2, local copies, waits for them, and re-layouts, gathered(): return result.reshape(top, rows, 2, hidden).transpose(1, 0, 2, 3)  3.68 us

profile of v2, /device:TPU:3, one launch (start us, length us, event | category | flops | bytes accessed | tf_op | source)
XLA Modules:
  0.0 83.0 jit_solution(17543973325921757889)
XLA Ops:
  0.0 79.3 %shard_map.73 = bf16[256,1536]{1,0:T(8,128)(2,1)} custom-call(s32[2]{0:T(128)} %seed_hbm.1, bf16[64,2880]{1,0:T(8,128)(2,1)} %tokens.1, s32[4,64]{1,0:T(4,128)} %bitcast.7, bf16[8,2880]{1,0:T(8,128)(2,1)} %bitcast.6, f32[1,8]{1,0:T(1,128)} %bitcast.8, bf16[1,2880,768]{2,1,0:T(8,128)(2,1)} %gate.1, bf16[1,2880,768]{2,1,0:T(8,128)(2,1)} %up.1), custom_call_target="tpu_custom_call" | custom-call | flops 9059696640 | bytes 8847360 | tf_op jit(solution)/shard_map/pallas_call | solution.py:437
  79.3 2.3 %reshape.3 = bf16[4,64,2,768]{3,2,1,0:T(2,128)(2,1)S(1)} reshape(bf16[256,1536]{1,0:T(8,128)(2,1)} %shard_map.73) | data formatting | bytes 1572864 | tf_op jit(solution)/shard_map/reshape | solution.py:471
  81.6 1.4 %copy.10 = bf16[4,64,2,768]{3,2,0,1:T(2,128)(2,1)} copy(bf16[4,64,2,768]{3,2,1,0:T(2,128)(2,1)S(1)} %reshape.3) | data formatting | bytes 1572864 | tf_op jit(solution)/shard_map/reshape | solution.py:471

commit v3 on v2

--- a/solution.py
+++ b/solution.py
@@ -130,6 +130,7 @@
 
 
 Z, X, C = 4, 2, 2
+PIECES = 2
 ROW = X * C
 MESH = pl.DeviceIdType.MESH
 
@@ -191,7 +192,7 @@
     load.wait()
     pl.semaphore_wait(barrier, count - 1)
 
-    cut = rows // 2
+    cut = rows // PIECES
 
     def pass_on(slot, piece, way, target):
         block = held.at[slot, pl.ds(piece * cut, cut)]
@@ -211,7 +212,7 @@
             device_id={"exp": slot}, device_id_type=MESH,
         )
 
-    for piece in range(2):
+    for piece in range(PIECES):
         @pl.when(z < Z - 1)
         def _(piece=piece):
             pass_on(me, piece, 0, me + ROW).start()
@@ -261,17 +262,17 @@
 
             pass_on(slot, piece, 3, sibling).start()
 
-        @pl.when((above == 2) & (z == 1))
-        def _():
-            pass_on(me - ROW, piece, 2, beside).start()
-
-        @pl.when((above == 2) & (z == Z - 2))
-        def _():
-            pass_on(me + ROW, piece, 2, beside).start()
-
         across = chip_row(step) * ROW + (1 - x) * C + c
         arrived(across, piece)
         pass_on(across, piece, 3, sibling).start()
+
+        @pl.when((step == 0) & (z == 0))
+        def _():
+            pass_on(across, piece, 0, me + ROW).start()
+
+        @pl.when((step == 0) & (z == Z - 1))
+        def _():
+            pass_on(across, piece, 1, me - ROW).start()
 
     for copy in small:
         copy.wait()
@@ -291,27 +292,17 @@
         ref[rest:, :] = jnp.zeros((ref.shape[0] - rest, hidden), jnp.bfloat16)
         for piece in range(3):
             ref[rest + piece * noisy : rest + (piece + 1) * noisy, :] = part
-    relay(0, 0)
     load_g.wait()
     load_u.wait()
     gt[0:rest, :] = wg[whole:, :]
     ut[0:rest, :] = wu[whole:, :]
 
     scale = NOISE / math.sqrt(width)
-    batch = ROW * rows
+    batch = C * rows
     tile = 256
 
-    def visit(step, carry):
-        @pl.when(step > 0)
-        def _():
-            relay(step, 0)
-
-        relay(step, 1)
-        base = chip_row(step) * ROW
-        for piece in range(2):
-            arrived(base + x * C + 1 - c, piece)
-            arrived(base + (1 - x) * C + 1 - c, piece)
-        values = held[pl.ds(base, ROW)].reshape(batch, width)
+    def compute(base):
+        values = held[pl.ds(base, C)].reshape(batch, width)
         projected = lax.dot_general(
             values, left[...], (((1,), (1,)), ((), ())), preferred_element_type=jnp.float32
         )
@@ -328,24 +319,62 @@
 
         def columns(n, carry):
             at = pl.ds(pl.multiple_of(n * tile, tile), tile)
-            start = held[pl.ds(base, ROW), :, 0:whole].reshape(batch, whole)
+            start = held[pl.ds(base, C), :, 0:whole].reshape(batch, whole)
             g = jnp.dot(start, wg[0:whole, at], preferred_element_type=jnp.float32)
             g = g + jnp.dot(end, gt[:, at], preferred_element_type=jnp.float32)
             u = jnp.dot(start, wu[0:whole, at], preferred_element_type=jnp.float32)
             u = u + jnp.dot(end, ut[:, at], preferred_element_type=jnp.float32)
             value = (g * jax.nn.sigmoid(ALPHA * g) * (u + 1.0)).astype(jnp.bfloat16)
-            act[pl.ds(base, ROW), :, at] = value.reshape(ROW, rows, tile)
+            act[pl.ds(base, C), :, at] = value.reshape(C, rows, tile)
             return carry
 
         lax.fori_loop(0, hidden // tile, columns, 0)
 
-        @pl.when(step > 0)
-        def _():
-            for other in range(ROW):
+    def column(row):
+        @pl.when((row >= 0) & (row < Z))
+        def _():
+            base = row * ROW + x * C
+            for piece in range(PIECES):
+                arrived(base + 1 - c, piece)
+            compute(base)
+            for other in range(C):
                 give_back(base + other).start()
+
+    def visit(step, carry):
+        def forward(piece, carry):
+            relay(step, piece)
+            return carry
+
+        lax.fori_loop(0, PIECES, forward, 0)
+        inward = 1 - 2 * (z // 2)
+        column(z + inward * (step + 1))
+        column(z - inward * (step + 1))
+        base = chip_row(step) * ROW + (1 - x) * C
+        for piece in range(PIECES):
+            arrived(base + 1 - c, piece)
+        compute(base)
         return carry
 
+    for piece in range(PIECES):
+        arrived(sibling, piece)
+    compute(me - c)
     lax.fori_loop(0, Z, visit, 0)
+    def far(step):
+        for other in range(C):
+            give_back(chip_row(step) * ROW + (1 - x) * C + other).start()
+
+    middle = (z // 2 + z) % 2
+
+    @pl.when(middle == 0)
+    def _():
+        for step in (3, 2, 1):
+            far(step)
+
+    @pl.when(middle == 1)
+    def _():
+        for step in (2, 1, 3):
+            far(step)
+
     give_back(beside).start()
     give_back(beside + 1 - 2 * c).start()
     give_back(sibling).start()
@@ -405,7 +434,7 @@
     lax.fori_loop(1, count, sent, 0)
 
     def passed(k, carry):
-        zo, piece = k // 2, k % 2
+        zo, piece = k // PIECES, k % PIECES
         slot = zo * ROW + x * C + c
 
         @pl.when((zo <= z) & (z < Z - 1))
@@ -416,12 +445,23 @@
         def _():
             pass_on(slot, piece, 1, me - ROW).wait_send()
 
-        pass_on(slot, piece, 2, beside).wait_send()
+        @pl.when(((z != 1) | (zo != 0)) & ((z != Z - 2) | (zo != Z - 1)))
+        def _():
+            pass_on(slot, piece, 2, beside).wait_send()
+
+        @pl.when((zo == 0) & (z == 0))
+        def _():
+            pass_on(zo * ROW + (1 - x) * C + c, piece, 0, me + ROW).wait_send()
+
+        @pl.when((zo == Z - 1) & (z == Z - 1))
+        def _():
+            pass_on(zo * ROW + (1 - x) * C + c, piece, 1, me - ROW).wait_send()
+
         pass_on(slot, piece, 3, sibling).wait_send()
         pass_on(zo * ROW + (1 - x) * C + c, piece, 3, sibling).wait_send()
         return carry
 
-    lax.fori_loop(0, 2 * Z, passed, 0)
+    lax.fori_loop(0, PIECES * Z, passed, 0)
 
 
 def gathered(tokens, routes, router_weight, router_bias, member_seeds, gate_weight, up_weight):
@@ -451,8 +491,8 @@
             pltpu.VMEM((noisy, width), half_dtype),
             pltpu.VMEM((count, rows, hidden), half_dtype),
             pltpu.VMEM((2, expert_count, rows, hidden), half_dtype),
-            pltpu.SemaphoreType.DMA((count, 2, 4)),
-            pltpu.SemaphoreType.DMA((count, 2)),
+            pltpu.SemaphoreType.DMA((count, PIECES, 4)),
+            pltpu.SemaphoreType.DMA((count, PIECES)),
             pltpu.SemaphoreType.DMA((count,)),
             pltpu.SemaphoreType.DMA((count,)),
             pltpu.SemaphoreType.DMA((6,)),

time: 83.2 us -> 75.3 us (0.905)
  the two profiles are of different devices: /device:TPU:3 before, /device:TPU:9 now
where the time goes in v3:
time: 75.3 us; the launch traced here: 75.1 us
  Pallas kernels  71.5 us (95%)
  local copies, waits for them, and re-layouts  3.68 us (5%)
    pallas_call x1, Pallas kernels, gathered(): pl.pallas_call(functools.partial(fused, expert_count), out_shape=jax.Shap...  71.5 us
    reshape x2, local copies, waits for them, and re-layouts, gathered(): return result.reshape(top, rows, 2, hidden).transpose(1, 0, 2, 3)  3.68 us

profile of v3, /device:TPU:9, one launch (start us, length us, event | category | flops | bytes accessed | tf_op | source)
XLA Modules:
  0.0 75.1 jit_solution(11964617056981045302)
XLA Ops:
  0.0 71.5 %shard_map.73 = bf16[256,1536]{1,0:T(8,128)(2,1)} custom-call(s32[2]{0:T(128)} %seed_hbm.1, bf16[64,2880]{1,0:T(8,128)(2,1)} %tokens.1, s32[4,64]{1,0:T(4,128)} %bitcast.7, bf16[8,2880]{1,0:T(8,128)(2,1)} %bitcast.6, f32[1,8]{1,0:T(1,128)} %bitcast.8, bf16[1,2880,768]{2,1,0:T(8,128)(2,1)} %gate.1, bf16[1,2880,768]{2,1,0:T(8,128)(2,1)} %up.1), custom_call_target="tpu_custom_call" | custom-call | flops 9059696640 | bytes 8847360 | tf_op jit(solution)/shard_map/pallas_call | solution.py:477
  71.5 2.3 %reshape.3 = bf16[4,64,2,768]{3,2,1,0:T(2,128)(2,1)S(1)} reshape(bf16[256,1536]{1,0:T(8,128)(2,1)} %shard_map.73) | data formatting | bytes 1572864 | tf_op jit(solution)/shard_map/reshape | solution.py:511
  73.7 1.4 %copy.10 = bf16[4,64,2,768]{3,2,0,1:T(2,128)(2,1)} copy(bf16[4,64,2,768]{3,2,1,0:T(2,128)(2,1)S(1)} %reshape.3) | data formatting | bytes 1572864 | tf_op jit(solution)/shard_map/reshape | solution.py:511

commit v4 on v3

--- a/solution.py
+++ b/solution.py
@@ -337,8 +337,17 @@
             for piece in range(PIECES):
                 arrived(base + 1 - c, piece)
             compute(base)
-            for other in range(C):
-                give_back(base + other).start()
+
+            @pl.when(row // 2 != z // 2)
+            def _():
+                for other in range(C):
+                    give_back(base + other).start()
+
+    def far(step):
+        for other in range(C):
+            give_back(chip_row(step) * ROW + (1 - x) * C + other).start()
+
+    middle = (z // 2 + z) % 2
 
     def visit(step, carry):
         def forward(piece, carry):
@@ -353,28 +362,33 @@
         for piece in range(PIECES):
             arrived(base + 1 - c, piece)
         compute(base)
+
+        @pl.when(step == 2)
+        def _():
+            far(1)
+
+            @pl.when(middle == 0)
+            def _():
+                far(2)
+
         return carry
 
     for piece in range(PIECES):
         arrived(sibling, piece)
     compute(me - c)
     lax.fori_loop(0, Z, visit, 0)
-    def far(step):
-        for other in range(C):
-            give_back(chip_row(step) * ROW + (1 - x) * C + other).start()
-
-    middle = (z // 2 + z) % 2
-
     @pl.when(middle == 0)
     def _():
-        for step in (3, 2, 1):
-            far(step)
+        far(3)
 
     @pl.when(middle == 1)
     def _():
-        for step in (2, 1, 3):
-            far(step)
-
+        far(2)
+        far(3)
+
+    near_row = z + 1 - 2 * (z % 2)
+    for other in range(C):
+        give_back(near_row * ROW + x * C + other).start()
     give_back(beside).start()
     give_back(beside + 1 - 2 * c).start()
     give_back(sibling).start()
@@ -399,16 +413,31 @@
     peak = functools.reduce(jnp.maximum, chosen)
     grown = [jnp.exp(v - peak) for v in chosen]
     total = sum(grown[1:], grown[0])
-    weights = jnp.concatenate([v / total for v in grown], axis=0)
-    place = lax.broadcasted_iota(jnp.int32, (rows, expert_count * rows), 1).astype(jnp.float32)
-    token = lax.broadcasted_iota(jnp.int32, (rows, expert_count * rows), 0).astype(jnp.float32)
-    pick = jnp.concatenate(
-        [
-            jnp.where(place == named[:, j : j + 1] * rows + token, 1.0, 0.0).astype(jnp.bfloat16)
-            for j in range(top)
-        ],
-        axis=0,
-    )
+    lines = rows * top * 2
+    line = lax.broadcasted_iota(jnp.int32, (lines, rows), 0)
+    spread = jnp.where(
+        line // (2 * top) == lax.broadcasted_iota(jnp.int32, (lines, rows), 1), 1.0, 0.0
+    ).astype(jnp.bfloat16)
+    line = lax.broadcasted_iota(jnp.int32, (lines, 1), 0)
+    weights = jnp.zeros((lines, 1), jnp.float32)
+    choice = jnp.zeros((lines, 1), jnp.float32)
+    for j in range(top):
+        rest_j = grown[j] / total
+        columns_j = [named[:, j : j + 1].astype(jnp.bfloat16)]
+        for _ in range(3):
+            piece = rest_j.astype(jnp.bfloat16)
+            rest_j = rest_j - piece.astype(jnp.float32)
+            columns_j.append(piece)
+        wide = jnp.dot(
+            spread, jnp.concatenate(columns_j, axis=1), preferred_element_type=jnp.float32
+        )
+        mine = (line // 2) % top == j
+        choice = jnp.where(mine, wide[:, 0:1], choice)
+        weights = jnp.where(mine, wide[:, 1:2] + wide[:, 2:3] + wide[:, 3:4], weights)
+    source = (line % 2) * (expert_count * rows) + line // (2 * top)
+    source = source + choice.astype(jnp.int32) * rows
+    place = lax.broadcasted_iota(jnp.int32, (lines, 2 * expert_count * rows), 1)
+    pick = jnp.where(place == source, 1.0, 0.0).astype(jnp.bfloat16)
 
     def take(k, carry):
         slot = (me + k) % count
@@ -420,11 +449,10 @@
         return carry
 
     lax.fori_loop(1, count, take, 0)
-    for h in range(2):
-        found = jnp.dot(
-            pick, back[h].reshape(expert_count * rows, hidden), preferred_element_type=jnp.float32
-        )
-        out[:, h * hidden : (h + 1) * hidden] = (found * weights).astype(jnp.bfloat16)
+    found = jnp.dot(
+        pick, back[...].reshape(2 * expert_count * rows, hidden), preferred_element_type=jnp.float32
+    )
+    out[...] = (found * weights).astype(jnp.bfloat16).reshape(rows * top, 2, hidden)
 
     def sent(k, carry):
         slot = (me + k) % count
@@ -476,7 +504,7 @@
     half_dtype = jnp.bfloat16
     result = pl.pallas_call(
         functools.partial(fused, expert_count),
-        out_shape=jax.ShapeDtypeStruct((top * rows, 2 * hidden), half_dtype),
+        out_shape=jax.ShapeDtypeStruct((top * rows, 2, hidden), half_dtype),
         in_specs=[anywhere] * 3 + [vmem] + [anywhere] * 3,
         out_specs=vmem,
         scratch_shapes=[
@@ -508,7 +536,7 @@
     )(
         member_seeds, tokens, routes.T, router_weight.T, router_bias[None, :], gate_weight, up_weight
     )
-    return result.reshape(top, rows, 2, hidden).transpose(1, 0, 2, 3)
+    return result.reshape(rows, top, 2, hidden)
 
 
 def fits(mesh, tokens, routes, router_weight, member_seeds, gate_weight):

time: 75.3 us -> 70.4 us (0.935)
  the two profiles are of different devices: /device:TPU:9 before, /device:TPU:1 now
where the time goes in v4:
time: 70.4 us; the launch traced here: 70.2 us
  Pallas kernels  67.7 us (96%)
  local copies, waits for them, and re-layouts  2.55 us (4%)
    pallas_call x1, Pallas kernels, gathered(): pl.pallas_call(functools.partial(fused, expert_count), out_shape=jax.Shap...  67.7 us
    unnamed x1, local copies, waits for them, and re-layouts  2.55 us

profile of v4, /device:TPU:1, one launch (start us, length us, event | category | flops | bytes accessed | tf_op | source)
XLA Modules:
  0.0 70.2 jit_solution(2783992716948325277)
XLA Ops:
  0.0 67.7 %shard_map.73 = bf16[256,2,768]{2,1,0:T(2,128)(2,1)} custom-call(s32[2]{0:T(128)} %seed_hbm.1, bf16[64,2880]{1,0:T(8,128)(2,1)} %tokens.1, s32[4,64]{1,0:T(4,128)} %bitcast.6, bf16[8,2880]{1,0:T(8,128)(2,1)} %bitcast.5, f32[1,8]{1,0:T(1,128)} %bitcast.7, bf16[1,2880,768]{2,1,0:T(8,128)(2,1)} %gate.1, bf16[1,2880,768]{2,1,0:T(8,128)(2,1)} %up.1), custom_call_target="tpu_custom_call" | custom-call | flops 9059696640 | bytes 8847360 | tf_op jit(solution)/shard_map/pallas_call | solution.py:505
  67.7 2.6 %copy.9 = bf16[64,4,2,768]{3,2,1,0:T(2,128)(2,1)} copy(bf16[64,4,2,768]{3,2,1,0:T(2,128)(2,1)} %bitcast.4) | data formatting | bytes 1572864
